TPU v7x, 128 devices: a whole 4x4x4 slice. The times are simulated.
128 devices in a mesh: cells: 32 (over y, z, core), edges: 4 (over x).
Axes of the slice: x: 4, y: 4, z: 4, core: 2. Of those that a mesh axis runs over, the one named last changes fastest.
Arguments:
- cells_in: bfloat16 [262144, 768], P(('cells', 'edges')), may hold values from -6 to 6
- w_in: bfloat16 [768, 768], replicated, may hold values from -0.21875 to 0.21875
- w_edge: bfloat16 [768, 768], replicated, may hold values from -0.21875 to 0.21875
- w_out: bfloat16 [768, 768], replicated, may hold values from -0.21875 to 0.21875
- cotangent: bfloat16 [262144, 768], P(('cells', 'edges')), may hold values from -6 to 6
- cell_row: int32 [262144], P(('cells', 'edges')), may hold values from 0 to 255
- send_slot: int32 [2, 262144], P(None, ('cells', 'edges')), may hold values from 0 to 127, as said below
- recv_target: int32 [128, 128], P(('cells', 'edges')), may hold values from 0 to 256, as said below
Outputs:
- layer_out: bfloat16 [262144, 768], P(('cells', 'edges'))
- grad_cells: bfloat16 [262144, 768], P(('cells', 'edges'))
- grad_win: float32 [768, 768], replicated
- grad_wedge: float32 [768, 768], replicated
- grad_wout: float32 [768, 768], replicated
Inputs may be any that keep to these rules, and one draw needn't show every extreme that they name: send_slot[k, i] is a slot of the device holding cell i; slot j goes to the device at place j // 32 of that device's group of 4, and every slot that a cell names is live at that owner. recv_target[d, e * 32 + c] is the hyperedge among those device d owns that slot (d % 4) * 32 + c of the device at place e of d's group feeds, or 256 for a slot that carries nothing; live slots of one source to one owner come first, each source has at least one live slot to every owner of its group, and some owner of each group receives 32 live slots from every source of the group. cell_row[i] is the row of cell i among the rows of the device holding it.
All inputs are finite; a program needn't handle non-finite values.
Results may differ from a plain program's by a relative error of at most 0.015.
Values may be sent and summed in bfloat16 or wider, within the bound.
A program may use at most 128 MiB of HBM per device.

v0:
```python
import jax
import jax.numpy as jnp
from jax import lax
from jax.sharding import PartitionSpec as P

ROWS_DEV = 256
HE_DEV = 256


def contract_rows(left, right):
    return lax.dot_general(
        left, right, (((0,), (0,)), ((), ())), preferred_element_type=jnp.float32
    )


def times_transpose(left, right):
    return lax.dot_general(
        left, right, (((1,), (1,)), ((), ())), preferred_element_type=jnp.float32
    )


def gather_edges(target_wide, received):
    return lax.dot_general(
        target_wide,
        received,
        (((0,), (0,)), ((), ())),
        precision=lax.Precision.HIGHEST,
        preferred_element_type=jnp.float32,
    )


def per_device(cells_in, w_in, w_edge, w_out, cotangent, cell_row, send_slot, recv_target):
    n_edges = lax.axis_size("edges")
    slots = recv_target.shape[1]
    capacity = slots // n_edges
    width = cells_in.shape[1]
    slot_ids = lax.broadcasted_iota(jnp.int32, (1, slots), 1)
    slot_hot = (send_slot[0][:, None] == slot_ids).astype(jnp.bfloat16) + (
        send_slot[1][:, None] == slot_ids
    ).astype(jnp.bfloat16)
    row_ids = lax.broadcasted_iota(jnp.int32, (1, ROWS_DEV), 1)
    row_hot = (cell_row[:, None] == row_ids).astype(jnp.bfloat16)
    edge_ids = lax.broadcasted_iota(jnp.int32, (1, HE_DEV), 1)
    target_match = recv_target[0][:, None] == edge_ids
    target_wide = target_match.astype(jnp.float32)
    target_narrow = target_match.astype(jnp.bfloat16)
    preact = jnp.dot(cells_in, w_in, preferred_element_type=jnp.float32)
    message = jax.nn.silu(preact).astype(jnp.bfloat16)
    slot_sums = contract_rows(slot_hot, message)
    slot_counts = jnp.sum(slot_hot.astype(jnp.float32), axis=0)
    got_sums, got_counts = (
        lax.all_to_all(
            slot_sums.reshape(n_edges, capacity, width).astype(jnp.bfloat16),
            "edges",
            split_axis=0,
            concat_axis=0,
            tiled=True,
        ).astype(jnp.float32),
        lax.all_to_all(
            slot_counts.reshape(n_edges, capacity).astype(jnp.bfloat16),
            "edges",
            split_axis=0,
            concat_axis=0,
            tiled=True,
        ).astype(jnp.float32),
    )
    edge_sums = gather_edges(target_wide, got_sums.reshape(slots, width))
    edge_counts = jnp.dot(got_counts.reshape(slots), target_wide, precision=lax.Precision.HIGHEST)
    row_sums = contract_rows(row_hot, message)
    row_counts = jnp.sum(row_hot.astype(jnp.float32), axis=0)
    counts_all = jnp.concatenate([row_counts, edge_counts])
    means = (jnp.concatenate([row_sums, edge_sums], axis=0) / (counts_all + 1.0)[:, None]).astype(
        jnp.bfloat16
    )
    hyper_out = jnp.dot(means, w_edge, preferred_element_type=jnp.float32).astype(jnp.bfloat16)
    reply = jnp.dot(target_narrow, hyper_out[ROWS_DEV:], preferred_element_type=jnp.float32).astype(
        jnp.bfloat16
    )
    returned = lax.all_to_all(
        reply.reshape(n_edges, capacity, width), "edges", split_axis=0, concat_axis=0, tiled=True
    )
    mixed = (
        jnp.dot(row_hot, hyper_out[:ROWS_DEV], preferred_element_type=jnp.float32)
        + jnp.dot(slot_hot, returned.reshape(slots, width), preferred_element_type=jnp.float32)
    ).astype(jnp.bfloat16)
    layer_out = (
        cells_in.astype(jnp.float32) + jnp.dot(mixed, w_out, preferred_element_type=jnp.float32)
    ).astype(jnp.bfloat16)
    grad_mixed = times_transpose(cotangent, w_out).astype(jnp.bfloat16)
    grad_wout = contract_rows(mixed, cotangent)
    slot_grads = contract_rows(slot_hot, grad_mixed)
    got_grads = lax.all_to_all(
        slot_grads.reshape(n_edges, capacity, width).astype(jnp.bfloat16),
        "edges",
        split_axis=0,
        concat_axis=0,
        tiled=True,
    ).astype(jnp.float32)
    edge_grads = gather_edges(target_wide, got_grads.reshape(slots, width))
    row_grads = contract_rows(row_hot, grad_mixed)
    hyper_grads = jnp.concatenate([row_grads, edge_grads], axis=0).astype(jnp.bfloat16)
    grad_wedge = contract_rows(means, hyper_grads)
    grad_means = (times_transpose(hyper_grads, w_edge) / (counts_all + 1.0)[:, None]).astype(
        jnp.bfloat16
    )
    answer = jnp.dot(
        target_narrow, grad_means[ROWS_DEV:], preferred_element_type=jnp.float32
    ).astype(jnp.bfloat16)
    answered = lax.all_to_all(
        answer.reshape(n_edges, capacity, width), "edges", split_axis=0, concat_axis=0, tiled=True
    )
    grad_message = jnp.dot(
        row_hot, grad_means[:ROWS_DEV], preferred_element_type=jnp.float32
    ) + jnp.dot(slot_hot, answered.reshape(slots, width), preferred_element_type=jnp.float32)
    sigma = jax.nn.sigmoid(preact)
    grad_pre = (grad_message * sigma * (1.0 + preact * (1.0 - sigma))).astype(jnp.bfloat16)
    grad_cells = (cotangent.astype(jnp.float32) + times_transpose(grad_pre, w_in)).astype(
        jnp.bfloat16
    )
    grad_win = contract_rows(cells_in, grad_pre)
    summed_win, summed_wedge, summed_wout = lax.psum(
        (grad_win, grad_wedge, grad_wout), ("cells", "edges")
    )
    return (layer_out, grad_cells, summed_win, summed_wedge, summed_wout)


def solution(mesh):
    placed = (
        P(("cells", "edges"), None),
        P(),
        P(),
        P(),
        P(("cells", "edges"), None),
        P(("cells", "edges")),
        P(None, ("cells", "edges")),
        P(("cells", "edges"), None),
    )
    return jax.shard_map(
        per_device,
        mesh=mesh,
        in_specs=placed,
        out_specs=(P(("cells", "edges"), None), P(("cells", "edges"), None), P(), P(), P()),
        check_vma=False,
    )
```

profile of v0, /device:TPU:1, one launch (start us, length us, event | category | flops | bytes accessed | tf_op | source)
XLA Modules:
  0.0 273.3 jit_solution(4017949495651273477)
XLA Ops:
  9.9 4.8 %all-to-all-start.1 = ((bf16[4,1,32]{2,1,0:T(2,128)(2,1)}), bf16[4,1,32]{2,1,0:T(2,128)(2,1)S(1)}, u32[]{:S(2)}, u32[]{:S(2)}) async-start(bf16[4,1,32]{2,1,0:T(2,128)(2,1)} %convert_element_type.103), calls=%async_computation.1 | async-start | bytes 4096 | tf_op jit(solution)/shard_map/all_to_all | solution.py:59
  14.7 4.9 %convolution_convert_fusion = bf16[2048,768]{1,0:T(8,128)(2,1)S(1)} fusion(bf16[2048,768]{1,0:T(8,128)(2,1)} %param.12, bf16[768,768]{1,0:T(8,128)(2,1)} %param.11), kind=kOutput, calls=%fused_computation.6 | convolution fusion | flops 2417491968 | bytes 7471104 | tf_op jit(solution)/shard_map/dot_general | solution.py:17
  19.6 2.2 convolution_convert_fusion.4
  21.8 2.0 fusion.6
  23.9 4.9 %multiply_convert_fusion.1 = (bf16[2048,768]{1,0:T(8,128)(2,1)S(1)}, f32[2048,768]{1,0:T(8,128)}) fusion(bf16[2048,768]{1,0:T(8,128)(2,1)S(1)} %copy-done.8, bf16[768,768]{1,0:T(8,128)(2,1)S(1)} %copy-done), kind=kOutput, calls=%fused_computation.4 | convolution fusion | flops 2423783424 | bytes 13762560 | tf_op jit(solution)/shard_map/dot_general | solution.py:47
  28.8 2.2 convolution_convert_fusion.6
  31.0 2.2 fusion.4
  33.5 4.2 %all-to-all-start.3 = ((bf16[4,32,768]{2,1,0:T(8,128)(2,1)}), bf16[4,32,768]{2,1,0:T(8,128)(2,1)S(1)}, u32[]{:S(2)}, u32[]{:S(2)}) async-start(bf16[4,32,768]{2,1,0:T(8,128)(2,1)} %bitcast.8), calls=%async_computation.3 | async-start | bytes 393216 | tf_op jit(solution)/shard_map/all_to_all | solution.py:92
  38.1 4.9 %all-to-all-done.3 = bf16[4,32,768]{2,1,0:T(8,128)(2,1)S(1)} async-done(((bf16[4,32,768]{2,1,0:T(8,128)(2,1)}), bf16[4,32,768]{2,1,0:T(8,128)(2,1)S(1)}, u32[]{:S(2)}, u32[]{:S(2)}) %all-to-all-start.3) | async-done | bytes 196640 | tf_op jit(solution)/shard_map/all_to_all | solution.py:92
  43.0 3.5 %all-to-all-start = ((bf16[4,32,768]{2,1,0:T(8,128)(2,1)}), bf16[4,32,768]{2,1,0:T(8,128)(2,1)S(1)}, u32[]{:S(2)}, u32[]{:S(2)}) async-start(bf16[4,32,768]{2,1,0:T(8,128)(2,1)} %bitcast.3), calls=%async_computation | async-start | bytes 393216 | tf_op jit(solution)/shard_map/all_to_all | solution.py:52
  48.7 3.2 %fusion = f32[2048,768]{1,0:T(8,128)} fusion(s32[2048]{0:T(1024)S(1)} %copy-done.5, bf16[512,768]{1,0:T(8,128)(2,1)S(1)} %divide_convert_fusion), kind=kOutput, calls=%fused_computation.9 | convolution fusion | flops 805830656 | bytes 6692864 | tf_op jit(solution)/shard_map/dot_general | solution.py:112
  53.3 2.2 convolution_convert_fusion.1
  55.5 2.3 fusion.27
  57.8 4.0 %all-to-all-start.4 = ((bf16[4,32,768]{2,1,0:T(8,128)(2,1)}), bf16[4,32,768]{2,1,0:T(8,128)(2,1)S(1)}, u32[]{:S(2)}, u32[]{:S(2)}) async-start(bf16[4,32,768]{2,1,0:T(8,128)(2,1)} %bitcast.10), calls=%async_computation.4 | async-start | bytes 393216 | tf_op jit(solution)/shard_map/all_to_all | solution.py:109
  61.8 3.3 %fusion.2 = f32[2048,768]{1,0:T(8,128)} fusion(s32[2048]{0:T(1024)S(1)} %copy-done.5, bf16[512,768]{1,0:T(8,128)(2,1)S(1)} %convolution_convert_fusion.1), kind=kOutput, calls=%fused_computation.11 | convolution fusion | flops 805830656 | bytes 6692864 | tf_op jit(solution)/shard_map/dot_general | solution.py:83
  67.0 3.4 %all-to-all-start.2 = ((bf16[4,32,768]{2,1,0:T(8,128)(2,1)}), bf16[4,32,768]{2,1,0:T(8,128)(2,1)S(1)}, u32[]{:S(2)}, u32[]{:S(2)}) async-start(bf16[4,32,768]{2,1,0:T(8,128)(2,1)} %bitcast.6), calls=%async_computation.2 | async-start | bytes 393216 | tf_op jit(solution)/shard_map/all_to_all | solution.py:79
  70.4 6.8 %multiply_convert_fusion = bf16[2048,768]{1,0:T(8,128)(2,1)S(1)} fusion(f32[2048,768]{1,0:T(8,128)} %get-tuple-element.31, f32[2048,768]{1,0:T(8,128)} %fusion, bf16[128,768]{1,0:T(8,128)(2,1)S(1)} %bitcast.50, s32[2048]{0:T(1024)S(1)} %bitcast.48, s32[2048]{0:T(1024)S(1)} %bitcast.43), kind=kOutput, calls=%fused_computation.1 | convolution fusion | flops 420478976 | bytes 15941632 | tf_op jit(solution)/shard_map/dot_general | solution.py:114
  79.0 4.1 %convolution_bitcast_fusion = f32[768,768]{0,1:T(8,128)} fusion(bf16[2048,768]{1,0:T(8,128)(2,1)S(1)} %multiply_convert_fusion, bf16[2048,768]{1,0:T(8,128)(2,1)S(1)} %copy-done.9), kind=kOutput, calls=%fused_computation.14 | convolution fusion | flops 2415919104 | bytes 8650752 | tf_op jit(solution)/shard_map/dot_general | solution.py:11
  83.1 3.7 %add_convert_fusion.2 = bf16[2048,768]{1,0:T(8,128)(2,1)S(1)} fusion(f32[2048,768]{1,0:T(8,128)} %fusion.2, bf16[128,768]{1,0:T(8,128)(2,1)S(1)} %bitcast.39, s32[2048]{0:T(1024)S(1)} %bitcast.49, s32[2048]{0:T(1024)S(1)} %bitcast.44), kind=kOutput, calls=%fused_computation.3 | convolution fusion | flops 407896064 | bytes 9650176 | tf_op jit(solution)/shard_map/dot_general | solution.py:84
  88.6 4.1 %fusion.44 = f32[768,768]{1,0:T(8,128)} fusion(bf16[2048,768]{1,0:T(8,128)(2,1)S(1)} %add_convert_fusion.2, bf16[2048,768]{1,0:T(8,128)(2,1)S(1)} %copy-done.7), kind=kOutput, calls=%fused_computation.61 | convolution fusion | flops 2415919104 | bytes 8650752 | tf_op jit(solution)/shard_map/dot_general | solution.py:11
  92.7 7.3 %add_convert_fusion = bf16[2048,768]{1,0:T(8,128)(2,1)} fusion(bf16[2048,768]{1,0:T(8,128)(2,1)} %param.12, bf16[2048,768]{1,0:T(8,128)(2,1)} %copy-done.13, bf16[768,768]{1,0:T(8,128)(2,1)S(1)} %copy-done), kind=kOutput, calls=%fused_computation | convolution fusion | flops 2420637696 | bytes 10616832 | tf_op jit(solution)/shard_map/dot_general | solution.py:17
  100.1 4.0 %add_convert_fusion.1 = bf16[2048,768]{1,0:T(8,128)(2,1)} fusion(bf16[2048,768]{1,0:T(8,128)(2,1)S(1)} %copy-done.10, bf16[2048,768]{1,0:T(8,128)(2,1)S(1)} %copy-done.2, bf16[768,768]{1,0:T(8,128)(2,1)S(1)} %copy-done.12), kind=kOutput, calls=%fused_computation.2 | convolution fusion | flops 2420637696 | bytes 10616832 | tf_op jit(solution)/shard_map/dot_general | solution.py:87
  104.0 155.3 %all-reduce.3.cloned.1.call-done = (f32[768,768]{0,1:T(8,128)}, f32[768,768]{1,0:T(8,128)}, f32[768,768]{1,0:T(8,128)}) async-done(((f32[768,768]{0,1:T(8,128)}, f32[768,768]{1,0:T(8,128)}, f32[768,768]{1,0:T(8,128)}), (f32[768,768]{0,1:T(8,128)}, f32[768,768]{1,0:T(8,128)}, f32[768,768]{1,0:T(8,128)})) %all-reduce.3.cloned.1.call-update) | async-done | bytes 7077904 | tf_op jit(solution)/shard_map/psum | solution.py:121
  259.4 3.2 %copy.19 = f32[768,768]{1,0:T(8,128)} copy(f32[768,768]{0,1:T(8,128)} %get-tuple-element.25) | data formatting | bytes 4718592
  (53 shorter events, 16.2 us)
Async XLA Ops:
  7.2 16.7 %copy-start = (bf16[768,768]{1,0:T(8,128)(2,1)S(1)}, bf16[768,768]{1,0:T(8,128)(2,1)}, u32[]{:S(2)}) copy-start(bf16[768,768]{1,0:T(8,128)(2,1)} %param.9) | copy-start | bytes 3538948
  9.9 23.6 %all-to-all-start.1 = ((bf16[4,1,32]{2,1,0:T(2,128)(2,1)}), bf16[4,1,32]{2,1,0:T(2,128)(2,1)S(1)}, u32[]{:S(2)}, u32[]{:S(2)}) async-start(bf16[4,1,32]{2,1,0:T(2,128)(2,1)} %convert_element_type.103), calls=%async_computation.1 | async-start | bytes 4096 | tf_op jit(solution)/shard_map/all_to_all | solution.py:59
  19.6 2.2 copy-start.5
  21.8 2.0 copy-start.8
  31.0 6.9 %copy-start.6 = (s32[1,128]{1,0:T(1,128)S(1)}, s32[1,128]{1,0:T(1,128)}, u32[]{:S(2)}) copy-start(s32[1,128]{1,0:T(1,128)} %param.15) | copy-start | bytes 1540
  31.0 15.9 %copy-start.11 = (bf16[768,768]{1,0:T(8,128)(2,1)S(1)}, bf16[768,768]{1,0:T(8,128)(2,1)}, u32[]{:S(2)}) copy-start(bf16[768,768]{1,0:T(8,128)(2,1)} %param.10) | copy-start | bytes 3538948
  33.5 9.4 %all-to-all-start.3 = ((bf16[4,32,768]{2,1,0:T(8,128)(2,1)}), bf16[4,32,768]{2,1,0:T(8,128)(2,1)S(1)}, u32[]{:S(2)}, u32[]{:S(2)}) async-start(bf16[4,32,768]{2,1,0:T(8,128)(2,1)} %bitcast.8), calls=%async_computation.3 | async-start | bytes 393216 | tf_op jit(solution)/shard_map/all_to_all | solution.py:92
  43.0 9.9 %all-to-all-start = ((bf16[4,32,768]{2,1,0:T(8,128)(2,1)}), bf16[4,32,768]{2,1,0:T(8,128)(2,1)S(1)}, u32[]{:S(2)}, u32[]{:S(2)}) async-start(bf16[4,32,768]{2,1,0:T(8,128)(2,1)} %bitcast.3), calls=%async_computation | async-start | bytes 393216 | tf_op jit(solution)/shard_map/all_to_all | solution.py:52
  48.7 4.6 %copy-start.14 = (f32[256,768]{1,0:T(8,128)S(1)}, f32[256,768]{1,0:T(8,128)}, u32[]{:S(2)}) copy-start(f32[256,768]{1,0:T(8,128)} %fusion.4) | copy-start | bytes 2359300
  53.3 2.2 copy-start.15
  57.8 9.2 %all-to-all-start.4 = ((bf16[4,32,768]{2,1,0:T(8,128)(2,1)}), bf16[4,32,768]{2,1,0:T(8,128)(2,1)S(1)}, u32[]{:S(2)}, u32[]{:S(2)}) async-start(bf16[4,32,768]{2,1,0:T(8,128)(2,1)} %bitcast.10), calls=%async_computation.4 | async-start | bytes 393216 | tf_op jit(solution)/shard_map/all_to_all | solution.py:109
  67.0 16.1 %all-to-all-start.2 = ((bf16[4,32,768]{2,1,0:T(8,128)(2,1)}), bf16[4,32,768]{2,1,0:T(8,128)(2,1)S(1)}, u32[]{:S(2)}, u32[]{:S(2)}) async-start(bf16[4,32,768]{2,1,0:T(8,128)(2,1)} %bitcast.6), calls=%async_computation.2 | async-start | bytes 393216 | tf_op jit(solution)/shard_map/all_to_all | solution.py:79
  70.4 189.0 %all-reduce.3.cloned.1.call-start = ((), (), s32[]{:S(2)}) async-start(), calls=%async_computation.5 | async-start | bytes 14155776 | tf_op jit(solution)/shard_map/psum | solution.py:121
  70.4 8.6 %copy-start.9 = (bf16[2048,768]{1,0:T(8,128)(2,1)S(1)}, bf16[2048,768]{1,0:T(8,128)(2,1)}, u32[]{:S(2)}) copy-start(bf16[2048,768]{1,0:T(8,128)(2,1)} %param.8) | copy-start | bytes 9437188
  77.3 1.7 copy-start.13
  83.1 5.4 %copy-start.7 = (bf16[2048,768]{1,0:T(8,128)(2,1)S(1)}, bf16[2048,768]{1,0:T(8,128)(2,1)}, u32[]{:S(2)}) copy-start(bf16[2048,768]{1,0:T(8,128)(2,1)} %param.12) | copy-start | bytes 9437188
  86.9 1.7 copy-start.1
  92.7 7.3 %copy-start.2 = (bf16[2048,768]{1,0:T(8,128)(2,1)S(1)}, bf16[2048,768]{1,0:T(8,128)(2,1)}, u32[]{:S(2)}) copy-start(bf16[2048,768]{1,0:T(8,128)(2,1)} %copy-done.1) | copy-start | bytes 9437188
  92.7 7.3 %copy-start.10 = (bf16[2048,768]{1,0:T(8,128)(2,1)S(1)}, bf16[2048,768]{1,0:T(8,128)(2,1)}, u32[]{:S(2)}) copy-start(bf16[2048,768]{1,0:T(8,128)(2,1)} %param.8) | copy-start | bytes 9437188
  92.7 7.3 %copy-start.12 = (bf16[768,768]{1,0:T(8,128)(2,1)S(1)}, bf16[768,768]{1,0:T(8,128)(2,1)}, u32[]{:S(2)}) copy-start(bf16[768,768]{1,0:T(8,128)(2,1)} %param.11) | copy-start | bytes 3538948
  259.4 3.2 %copy-start.4 = (f32[768,768]{1,0:T(8,128)S(1)}, f32[768,768]{1,0:T(8,128)}, u32[]{:S(2)}) copy-start(f32[768,768]{1,0:T(8,128)} %get-tuple-element.35) | copy-start | bytes 7077892
  262.6 2.5 copy-start.3
Sparse Core Ops, SparseCore 0:
  92.8 166.5 all-reduce.2
where the time goes:
time: 274 us; the launch traced here: 273 us
  waiting for transfers between devices  161 us (59%)
  matrix products  64.1 us (23%)
  starting transfers between devices  20.1 us (7%)
  between operations  14.2 us (5%)
  local copies, waits for them, and re-layouts  12.2 us (4%)
    psum x1, waiting for transfers between devices, per_device(): lax.psum((grad_win, grad_wedge, grad_wout), ('cells', 'edges'))  155 us
    dot_general x7, matrix products, contract_rows(): lax.dot_general(left, right, (((0,), (0,)), ((), ())), preferred_element_...  19.2 us
    dot_general x3, matrix products, times_transpose(): lax.dot_general(left, right, (((1,), (1,)), ((), ())), preferred_element_...  14 us
    unnamed x35, local copies, waits for them, and re-layouts  10.6 us
    dot_general x1, matrix products, per_device(): jnp.dot(slot_hot, answered.reshape(slots, width), preferred_element_type=...  6.85 us
  transfers between devices with their start and end apart: 6, of which 3 were waited for; matrix products, arithmetic and copies ran while one was open for 19% of the time, Pallas kernels for 0%

commit v1 on v0

--- a/solution.py
+++ b/solution.py
@@ -119,7 +119,7 @@
     )
     grad_win = contract_rows(cells_in, grad_pre)
     summed_win, summed_wedge, summed_wout = lax.psum(
-        (grad_win, grad_wedge, grad_wout), ("cells", "edges")
+        lax.psum((grad_win, grad_wedge, grad_wout), "cells"), "edges"
     )
     return (layer_out, grad_cells, summed_win, summed_wedge, summed_wout)
 

time: 274 us -> 375 us (1.37)
  waiting for transfers between devices: 161 us -> 261 us
    psum x1 -> x2, waiting for transfers between devices: 155 us -> 256 us  [the longest x1 131 us: per_device(): lax.psum(lax.psum((grad_win, grad_wedge, grad_wout), 'cells'), 'edges')]
  transfers between devices with their start and end apart: 6 -> 7, of which waited for: 3 -> 4; matrix products, arithmetic and copies ran while one was open for 19% -> 14% of each run, Pallas kernels for 0% -> 0%
where the time goes in v1:
time: 375 us; the launch traced here: 374 us
  waiting for transfers between devices  261 us (70%)
  matrix products  64.1 us (17%)
  starting transfers between devices  20.3 us (5%)
  between operations  14.2 us (4%)
  local copies, waits for them, and re-layouts  12.1 us (3%)
    psum x1, waiting for transfers between devices, per_device(): lax.psum(lax.psum((grad_win, grad_wedge, grad_wout), 'cells'), 'edges')  131 us
    psum x1, waiting for transfers between devices, per_device(): lax.psum((grad_win, grad_wedge, grad_wout), 'cells')  125 us
    dot_general x7, matrix products, contract_rows(): lax.dot_general(left, right, (((0,), (0,)), ((), ())), preferred_element_...  19.2 us
    dot_general x3, matrix products, times_transpose(): lax.dot_general(left, right, (((1,), (1,)), ((), ())), preferred_element_...  14 us
    unnamed x35, local copies, waits for them, and re-layouts  10.5 us
  transfers between devices with their start and end apart: 7, of which 4 were waited for; matrix products, arithmetic and copies ran while one was open for 14% of the time, Pallas kernels for 0%

profile of v1, /device:TPU:1, one launch (start us, length us, event | category | flops | bytes accessed | tf_op | source)
XLA Modules:
  0.0 373.9 jit_solution(9313760415776335758)
XLA Ops:
  9.9 4.8 %all-to-all-start.1 = ((bf16[4,1,32]{2,1,0:T(2,128)(2,1)}), bf16[4,1,32]{2,1,0:T(2,128)(2,1)S(1)}, u32[]{:S(2)}, u32[]{:S(2)}) async-start(bf16[4,1,32]{2,1,0:T(2,128)(2,1)} %convert_element_type.103), calls=%async_computation.1 | async-start | bytes 4096 | tf_op jit(solution)/shard_map/all_to_all | solution.py:59
  14.7 4.9 %convolution_convert_fusion = bf16[2048,768]{1,0:T(8,128)(2,1)S(1)} fusion(bf16[2048,768]{1,0:T(8,128)(2,1)} %param.12, bf16[768,768]{1,0:T(8,128)(2,1)} %param.11), kind=kOutput, calls=%fused_computation.6 | convolution fusion | flops 2417491968 | bytes 7471104 | tf_op jit(solution)/shard_map/dot_general | solution.py:17
  19.6 2.2 convolution_convert_fusion.4
  23.9 4.9 %multiply_convert_fusion.1 = (bf16[2048,768]{1,0:T(8,128)(2,1)S(1)}, f32[2048,768]{1,0:T(8,128)}) fusion(bf16[2048,768]{1,0:T(8,128)(2,1)S(1)} %copy-done.8, bf16[768,768]{1,0:T(8,128)(2,1)S(1)} %copy-done), kind=kOutput, calls=%fused_computation.4 | convolution fusion | flops 2423783424 | bytes 13762560 | tf_op jit(solution)/shard_map/dot_general | solution.py:47
  28.8 2.2 convolution_convert_fusion.6
  31.0 2.2 fusion.4
  33.5 4.2 %all-to-all-start.3 = ((bf16[4,32,768]{2,1,0:T(8,128)(2,1)}), bf16[4,32,768]{2,1,0:T(8,128)(2,1)S(1)}, u32[]{:S(2)}, u32[]{:S(2)}) async-start(bf16[4,32,768]{2,1,0:T(8,128)(2,1)} %bitcast.8), calls=%async_computation.3 | async-start | bytes 393216 | tf_op jit(solution)/shard_map/all_to_all | solution.py:92
  38.1 4.9 %all-to-all-done.3 = bf16[4,32,768]{2,1,0:T(8,128)(2,1)S(1)} async-done(((bf16[4,32,768]{2,1,0:T(8,128)(2,1)}), bf16[4,32,768]{2,1,0:T(8,128)(2,1)S(1)}, u32[]{:S(2)}, u32[]{:S(2)}) %all-to-all-start.3) | async-done | bytes 196640 | tf_op jit(solution)/shard_map/all_to_all | solution.py:92
  43.0 3.5 all-to-all-start
  48.7 3.2 fusion
  53.3 2.2 convolution_convert_fusion.1
  55.5 2.3 fusion.27
  57.8 4.0 %all-to-all-start.4 = ((bf16[4,32,768]{2,1,0:T(8,128)(2,1)}), bf16[4,32,768]{2,1,0:T(8,128)(2,1)S(1)}, u32[]{:S(2)}, u32[]{:S(2)}) async-start(bf16[4,32,768]{2,1,0:T(8,128)(2,1)} %bitcast.10), calls=%async_computation.4 | async-start | bytes 393216 | tf_op jit(solution)/shard_map/all_to_all | solution.py:109
  61.8 3.3 fusion.2
  67.0 3.4 all-to-all-start.2
  70.4 6.8 %multiply_convert_fusion = bf16[2048,768]{1,0:T(8,128)(2,1)S(1)} fusion(f32[2048,768]{1,0:T(8,128)} %get-tuple-element.34, f32[2048,768]{1,0:T(8,128)} %fusion, bf16[128,768]{1,0:T(8,128)(2,1)S(1)} %bitcast.50, s32[2048]{0:T(1024)S(1)} %bitcast.48, s32[2048]{0:T(1024)S(1)} %bitcast.43), kind=kOutput, calls=%fused_computation.1 | convolution fusion | flops 420478976 | bytes 15941632 | tf_op jit(solution)/shard_map/dot_general | solution.py:114
  79.0 4.1 %convolution_bitcast_fusion = f32[768,768]{0,1:T(8,128)} fusion(bf16[2048,768]{1,0:T(8,128)(2,1)S(1)} %multiply_convert_fusion, bf16[2048,768]{1,0:T(8,128)(2,1)S(1)} %copy-done.9), kind=kOutput, calls=%fused_computation.14 | convolution fusion | flops 2415919104 | bytes 8650752 | tf_op jit(solution)/shard_map/dot_general | solution.py:11
  83.1 3.7 %add_convert_fusion.2 = bf16[2048,768]{1,0:T(8,128)(2,1)S(1)} fusion(f32[2048,768]{1,0:T(8,128)} %fusion.2, bf16[128,768]{1,0:T(8,128)(2,1)S(1)} %bitcast.39, s32[2048]{0:T(1024)S(1)} %bitcast.49, s32[2048]{0:T(1024)S(1)} %bitcast.44), kind=kOutput, calls=%fused_computation.3 | convolution fusion | flops 407896064 | bytes 9650176 | tf_op jit(solution)/shard_map/dot_general | solution.py:84
  88.6 4.1 %fusion.44 = f32[768,768]{1,0:T(8,128)} fusion(bf16[2048,768]{1,0:T(8,128)(2,1)S(1)} %add_convert_fusion.2, bf16[2048,768]{1,0:T(8,128)(2,1)S(1)} %copy-done.7), kind=kOutput, calls=%fused_computation.61 | convolution fusion | flops 2415919104 | bytes 8650752 | tf_op jit(solution)/shard_map/dot_general | solution.py:11
  93.0 124.6 %all-reduce.5.cloned.1.call-done = (f32[768,768]{0,1:T(8,128)}, f32[768,768]{1,0:T(8,128)}, f32[768,768]{1,0:T(8,128)}) async-done(((f32[768,768]{0,1:T(8,128)}, f32[768,768]{1,0:T(8,128)}, f32[768,768]{1,0:T(8,128)}), (f32[768,768]{0,1:T(8,128)}, f32[768,768]{1,0:T(8,128)}, f32[768,768]{1,0:T(8,128)})) %all-reduce.5.cloned.1.call-update) | async-done | bytes 7077904 | tf_op jit(solution)/shard_map/psum | solution.py:122
  217.7 7.3 %add_convert_fusion = bf16[2048,768]{1,0:T(8,128)(2,1)} fusion(bf16[2048,768]{1,0:T(8,128)(2,1)} %param.12, bf16[2048,768]{1,0:T(8,128)(2,1)} %copy-done.13, bf16[768,768]{1,0:T(8,128)(2,1)S(1)} %copy-done), kind=kOutput, calls=%fused_computation | convolution fusion | flops 2420637696 | bytes 10616832 | tf_op jit(solution)/shard_map/dot_general | solution.py:17
  225.0 4.0 %add_convert_fusion.1 = bf16[2048,768]{1,0:T(8,128)(2,1)} fusion(bf16[2048,768]{1,0:T(8,128)(2,1)S(1)} %copy-done.10, bf16[2048,768]{1,0:T(8,128)(2,1)S(1)} %copy-done.2, bf16[768,768]{1,0:T(8,128)(2,1)S(1)} %copy-done.12), kind=kOutput, calls=%fused_computation.2 | convolution fusion | flops 2420637696 | bytes 10616832 | tf_op jit(solution)/shard_map/dot_general | solution.py:87
  229.0 130.9 %all-reduce.7.cloned.1.call-done = (f32[768,768]{0,1:T(8,128)}, f32[768,768]{1,0:T(8,128)}, f32[768,768]{1,0:T(8,128)}) async-done(((f32[768,768]{0,1:T(8,128)}, f32[768,768]{1,0:T(8,128)}, f32[768,768]{1,0:T(8,128)}), (f32[768,768]{0,1:T(8,128)}, f32[768,768]{1,0:T(8,128)}, f32[768,768]{1,0:T(8,128)})) %all-reduce.7.cloned.1.call-update) | async-done | bytes 7077904 | tf_op jit(solution)/shard_map/psum | solution.py:121
  359.9 3.2 copy.19
  (56 shorter events, 18.5 us)
Async XLA Ops:
  7.2 16.7 %copy-start = (bf16[768,768]{1,0:T(8,128)(2,1)S(1)}, bf16[768,768]{1,0:T(8,128)(2,1)}, u32[]{:S(2)}) copy-start(bf16[768,768]{1,0:T(8,128)(2,1)} %param.9) | copy-start | bytes 3538948
  9.9 23.6 %all-to-all-start.1 = ((bf16[4,1,32]{2,1,0:T(2,128)(2,1)}), bf16[4,1,32]{2,1,0:T(2,128)(2,1)S(1)}, u32[]{:S(2)}, u32[]{:S(2)}) async-start(bf16[4,1,32]{2,1,0:T(2,128)(2,1)} %convert_element_type.103), calls=%async_computation.1 | async-start | bytes 4096 | tf_op jit(solution)/shard_map/all_to_all | solution.py:59
  19.6 2.2 copy-start.5
  21.8 2.0 copy-start.8
  31.0 6.9 %copy-start.6 = (s32[1,128]{1,0:T(1,128)S(1)}, s32[1,128]{1,0:T(1,128)}, u32[]{:S(2)}) copy-start(s32[1,128]{1,0:T(1,128)} %param.15) | copy-start | bytes 1540
  31.0 15.9 %copy-start.11 = (bf16[768,768]{1,0:T(8,128)(2,1)S(1)}, bf16[768,768]{1,0:T(8,128)(2,1)}, u32[]{:S(2)}) copy-start(bf16[768,768]{1,0:T(8,128)(2,1)} %param.10) | copy-start | bytes 3538948
  33.5 9.4 %all-to-all-start.3 = ((bf16[4,32,768]{2,1,0:T(8,128)(2,1)}), bf16[4,32,768]{2,1,0:T(8,128)(2,1)S(1)}, u32[]{:S(2)}, u32[]{:S(2)}) async-start(bf16[4,32,768]{2,1,0:T(8,128)(2,1)} %bitcast.8), calls=%async_computation.3 | async-start | bytes 393216 | tf_op jit(solution)/shard_map/all_to_all | solution.py:92
  43.0 9.9 %all-to-all-start = ((bf16[4,32,768]{2,1,0:T(8,128)(2,1)}), bf16[4,32,768]{2,1,0:T(8,128)(2,1)S(1)}, u32[]{:S(2)}, u32[]{:S(2)}) async-start(bf16[4,32,768]{2,1,0:T(8,128)(2,1)} %bitcast.3), calls=%async_computation | async-start | bytes 393216 | tf_op jit(solution)/shard_map/all_to_all | solution.py:52
  48.7 4.6 %copy-start.14 = (f32[256,768]{1,0:T(8,128)S(1)}, f32[256,768]{1,0:T(8,128)}, u32[]{:S(2)}) copy-start(f32[256,768]{1,0:T(8,128)} %fusion.4) | copy-start | bytes 2359300
  53.3 2.2 copy-start.15
  57.8 9.2 %all-to-all-start.4 = ((bf16[4,32,768]{2,1,0:T(8,128)(2,1)}), bf16[4,32,768]{2,1,0:T(8,128)(2,1)S(1)}, u32[]{:S(2)}, u32[]{:S(2)}) async-start(bf16[4,32,768]{2,1,0:T(8,128)(2,1)} %bitcast.10), calls=%async_computation.4 | async-start | bytes 393216 | tf_op jit(solution)/shard_map/all_to_all | solution.py:109
  67.0 16.1 %all-to-all-start.2 = ((bf16[4,32,768]{2,1,0:T(8,128)(2,1)}), bf16[4,32,768]{2,1,0:T(8,128)(2,1)S(1)}, u32[]{:S(2)}, u32[]{:S(2)}) async-start(bf16[4,32,768]{2,1,0:T(8,128)(2,1)} %bitcast.6), calls=%async_computation.2 | async-start | bytes 393216 | tf_op jit(solution)/shard_map/all_to_all | solution.py:79
  70.4 147.2 %all-reduce.5.cloned.1.call-start = ((), (), s32[]{:S(2)}) async-start(), calls=%async_computation.5 | async-start | bytes 14155776 | tf_op jit(solution)/shard_map/psum | solution.py:122
  70.4 8.6 %copy-start.9 = (bf16[2048,768]{1,0:T(8,128)(2,1)S(1)}, bf16[2048,768]{1,0:T(8,128)(2,1)}, u32[]{:S(2)}) copy-start(bf16[2048,768]{1,0:T(8,128)(2,1)} %param.8) | copy-start | bytes 9437188
  77.3 1.7 copy-start.13
  83.1 5.4 %copy-start.7 = (bf16[2048,768]{1,0:T(8,128)(2,1)S(1)}, bf16[2048,768]{1,0:T(8,128)(2,1)}, u32[]{:S(2)}) copy-start(bf16[2048,768]{1,0:T(8,128)(2,1)} %param.12) | copy-start | bytes 9437188
  86.9 1.7 copy-start.1
  92.7 267.2 %all-reduce.7.cloned.1.call-start = ((), (), s32[]{:S(2)}) async-start(), calls=%async_computation.6 | async-start | bytes 14155776 | tf_op jit(solution)/shard_map/psum | solution.py:121
  217.6 7.3 %copy-start.2 = (bf16[2048,768]{1,0:T(8,128)(2,1)S(1)}, bf16[2048,768]{1,0:T(8,128)(2,1)}, u32[]{:S(2)}) copy-start(bf16[2048,768]{1,0:T(8,128)(2,1)} %copy-done.1) | copy-start | bytes 9437188
  217.7 7.3 %copy-start.10 = (bf16[2048,768]{1,0:T(8,128)(2,1)S(1)}, bf16[2048,768]{1,0:T(8,128)(2,1)}, u32[]{:S(2)}) copy-start(bf16[2048,768]{1,0:T(8,128)(2,1)} %param.8) | copy-start | bytes 9437188
  217.7 7.3 %copy-start.12 = (bf16[768,768]{1,0:T(8,128)(2,1)S(1)}, bf16[768,768]{1,0:T(8,128)(2,1)}, u32[]{:S(2)}) copy-start(bf16[768,768]{1,0:T(8,128)(2,1)} %param.11) | copy-start | bytes 3538948
  359.9 3.2 copy-start.4
  363.1 2.5 copy-start.3
Sparse Core Ops, SparseCore 0:
  92.8 124.7 all-reduce.4
  220.3 139.5 all-reduce.6
